TPU v7x, 32 devices: a whole 2x2x4 slice. The times are simulated.
32 devices in a mesh: tensor: 4 (over y, core), store: 8 (over z, x).
Axes of the slice: x: 2, y: 2, z: 4, core: 2. Of those that a mesh axis runs over, the one named last changes fastest.
Arguments:
- inputs: bfloat16 [256, 16, 28672], P('tensor', None, 'store'), may hold values from -6 to 6
- out_grads: bfloat16 [256, 16, 8192], P('tensor', None, 'store'), may hold values from -6 to 6
- proj_in: bfloat16 [28672, 128], P('store'), may hold values from -0.03125 to 0.03125
- proj_out: bfloat16 [8192, 128], P('store'), may hold values from -0.09375 to 0.09375
- inv_fisher: float32 [16384, 16384], P('store', 'tensor'), may hold values from -1 to 4
- store_grads: float32 [2048, 16384], P('store', 'tensor'), may hold values from -0.005859375 to 0.005859375
Outputs:
- scores: float32 [256, 2048], P('tensor', 'store')
All inputs are finite; a program needn't handle non-finite values.
Results may differ from a plain program's by a relative error of at most 0.0003.
Values sent between devices are 32-bit elements; how exact they have to be, the bound alone decides.
A program may use at most 128 MiB of HBM per device.

v0:
```python
import jax
import jax.numpy as jnp
from jax import lax
from jax.sharding import PartitionSpec as P

highest_precision = lax.Precision.HIGHEST


def outer_sums(grad_rows, act_rows):
    joined = jnp.einsum("etk,etj->ekj", grad_rows, act_rows, precision=highest_precision)
    return joined.reshape(joined.shape[0], joined.shape[1] * joined.shape[2])


def on_device(inputs, out_grads, proj_in, proj_out, inv_fisher, store_grads):
    examples_here = inputs.shape[0]
    tokens_each = inputs.shape[1]
    flat_inputs = inputs.reshape(examples_here * tokens_each, inputs.shape[2])
    flat_grads = out_grads.reshape(examples_here * tokens_each, out_grads.shape[2])
    act_part = jnp.dot(flat_inputs, proj_in, preferred_element_type=jnp.float32)
    grad_part = jnp.dot(flat_grads, proj_out, preferred_element_type=jnp.float32)
    act_full, grad_full = lax.psum((act_part, grad_part), "store")
    share_width = grad_full.shape[1] // lax.axis_size("store")
    grad_mine = lax.dynamic_slice_in_dim(
        grad_full, lax.axis_index("store") * share_width, share_width, 1
    )
    act_rows = act_full.reshape(examples_here, tokens_each, act_full.shape[1])
    grad_rows = grad_mine.reshape(examples_here, tokens_each, grad_mine.shape[1])
    local_grads = outer_sums(grad_rows, act_rows)
    precond_part = jnp.dot(
        lax.all_gather(local_grads, "tensor", axis=0, tiled=True),
        inv_fisher,
        precision=highest_precision,
        preferred_element_type=jnp.float32,
    )
    precond_whole = lax.psum(precond_part, "store")
    partial_scores = lax.dot_general(
        precond_whole,
        store_grads,
        (((1,), (1,)), ((), ())),
        precision=highest_precision,
        preferred_element_type=jnp.float32,
    )
    return lax.psum_scatter(partial_scores, "tensor", scatter_dimension=0, tiled=True)


def solution(mesh):
    placed = (
        P("tensor", None, "store"),
        P("tensor", None, "store"),
        P("store", None),
        P("store", None),
        P("store", "tensor"),
        P("store", "tensor"),
    )
    return jax.shard_map(
        on_device, mesh=mesh, in_specs=placed, out_specs=P("tensor", "store"), check_vma=False
    )
```

profile of v0, /device:TPU:0, one launch (start us, length us, event | category | flops | bytes accessed | tf_op | source)
XLA Modules:
  0.0 345.8 jit_solution(7406094724601756782)
XLA Ops:
  6.5 0.0 copy-start
  6.5 0.0 all-reduce.6.cloned.1.call-start
  6.5 0.0 copy-start.1
  6.5 6.3 %fusion.3 = f32[1024,128]{1,0:T(8,128)} fusion(bf16[1024,3584]{1,0:T(8,128)(2,1)} %bitcast.22, bf16[3584,128]{1,0:T(8,128)(2,1)} %param.8), kind=kOutput, calls=%fused_computation.5 | convolution fusion | flops 939524096 | bytes 8781824 | tf_op jit(solution)/shard_map/dot_general | solution.py:19
  12.8 0.0 copy-done
  12.8 0.0 copy-done.1
  12.8 1.6 fusion.2
  14.5 0.0 all-reduce.6.cloned.1.call-update
  14.5 0.0 all-gather.2.cloned.1.call-start
  14.5 81.2 %all-reduce.6.cloned.1.call-done = (f32[64,16,128]{2,1,0:T(8,128)}, f32[1024,128]{0,1:T(8,128)}) async-done(((f32[64,16,128]{2,1,0:T(8,128)}, f32[1024,128]{0,1:T(8,128)}), (f32[64,16,128]{2,1,0:T(8,128)}, f32[1024,128]{0,1:T(8,128)})) %all-reduce.6.cloned.1.call-update) | async-done | bytes 1048592 | tf_op jit(solution)/shard_map/psum | solution.py:21
  95.8 0.8 constant_dynamic-slice_fusion
  96.6 0.2 reshape.16
  96.8 2.0 fusion
  98.8 1.0 copy.12
  99.7 0.0 all-gather.2.cloned.1.call-update
  99.8 0.0 all-reduce.4.cloned.1.call-start
  99.8 22.1 %all-gather.2.cloned.1.call-done = f32[256,2048]{1,0:T(8,128)} async-done(((f32[64,2048]{1,0:T(8,128)}), f32[256,2048]{1,0:T(8,128)}) %all-gather.2.cloned.1.call-update) | async-done | bytes 2097168 | tf_op jit(solution)/shard_map/all_gather | solution.py:30
  121.9 34.0 %fusion.4 = f32[256,4096]{1,0:T(8,128)} fusion(f32[256,2048]{1,0:T(8,128)} %all-gather.2.cloned.1.call-done, f32[2048,4096]{1,0:T(8,128)} %param.10), kind=kOutput, calls=%fused_computation.6 | convolution fusion | flops 25769803776 | bytes 39845888 | tf_op jit(solution)/shard_map/dot_general | solution.py:29
  155.9 0.0 all-reduce.4.cloned.1.call-update
  155.9 0.2 reduce-scatter.2.cloned.1.call-start
  156.1 156.2 %all-reduce.4.cloned.1.call-done = f32[256,4096]{1,0:T(8,128)} async-done(((f32[256,4096]{1,0:T(8,128)}), f32[256,4096]{1,0:T(8,128)}) %all-reduce.4.cloned.1.call-update) | async-done | bytes 4194320 | tf_op jit(solution)/shard_map/psum | solution.py:35
  312.4 7.7 %fusion.5 = f32[256,256]{1,0:T(8,128)} fusion(f32[256,4096]{1,0:T(8,128)} %all-reduce.4.cloned.1.call-done, f32[256,4096]{1,0:T(8,128)} %param.11), kind=kOutput, calls=%fused_computation.7 | convolution fusion | flops 3221225472 | bytes 8650752 | tf_op jit(solution)/shard_map/dot_general | solution.py:36
  320.1 0.0 reduce-scatter.2.cloned.1.call-update
  320.1 19.2 %reduce-scatter.2.cloned.1.call-done = f32[64,256]{1,0:T(8,128)} async-done(((f32[256,256]{1,0:T(8,128)}), f32[64,256]{1,0:T(8,128)}) %reduce-scatter.2.cloned.1.call-update) | async-done | bytes 65552 | tf_op jit(solution)/shard_map/reduce_scatter | solution.py:43
Async XLA Ops:
  6.5 6.3 %copy-start = (bf16[64,16,1024]{2,1,0:T(8,128)(2,1)S(1)}, bf16[64,16,1024]{2,1,0:T(8,128)(2,1)}, u32[]{:S(2)}) copy-start(bf16[64,16,1024]{2,1,0:T(8,128)(2,1)} %param.7) | copy-start | bytes 6291460
  6.5 89.2 %all-reduce.6.cloned.1.call-start = ((), (), s32[]{:S(2)}) async-start(), calls=%async_computation.4 | async-start | bytes 2097152 | tf_op jit(solution)/shard_map/psum | solution.py:21
  6.5 6.3 %copy-start.1 = (bf16[1024,128]{1,0:T(8,128)(2,1)S(1)}, bf16[1024,128]{1,0:T(8,128)(2,1)}, u32[]{:S(2)}) copy-start(bf16[1024,128]{1,0:T(8,128)(2,1)} %param.9) | copy-start | bytes 786436
  14.5 107.4 %all-gather.2.cloned.1.call-start = ((), (), s32[]{:S(2)}) async-start(), calls=%async_computation.1 | async-start | bytes 2621440 | tf_op jit(solution)/shard_map/all_gather | solution.py:30
  99.8 212.6 %all-reduce.4.cloned.1.call-start = ((), (), s32[]{:S(2)}) async-start(), calls=%async_computation.2 | async-start | bytes 8388608 | tf_op jit(solution)/shard_map/psum | solution.py:35
  155.9 183.4 %reduce-scatter.2.cloned.1.call-start = ((), (), s32[]{:S(2)}) async-start(), calls=%async_computation.3 | async-start | bytes 327680 | tf_op jit(solution)/shard_map/reduce_scatter | solution.py:43
Sparse Core Ops, SparseCore 0:
  14.6 81.0 all-reduce.5
  99.9 21.9 all-gather.1
  156.0 156.2 all-reduce.3
  320.2 19.0 reduce-scatter.1
where the time goes:
time: 346 us
  waiting for transfers between devices  279 us (81%)
  matrix products  51.6 us (15%)
  between operations  13.1 us (4%)
    psum x1, waiting for transfers between devices, on_device(): precond_whole = lax.psum(precond_part, 'store')  156 us
    psum x1, waiting for transfers between devices, on_device(): act_full, grad_full = lax.psum((act_part, grad_part), 'store')  81.2 us
    dot_general x1, matrix products, on_device(): jnp.dot(lax.all_gather(local_grads, 'tensor', axis=0, tiled=True), inv_fi...  34 us
    all_gather x1, waiting for transfers between devices, on_device(): lax.all_gather(local_grads, 'tensor', axis=0, tiled=True)  22.1 us
    reduce_scatter x1, waiting for transfers between devices, on_device(): lax.psum_scatter(partial_scores, 'tensor', scatter_dimension=0, tiled=True)  19.2 us
    dot_general x1, matrix products, on_device(): lax.dot_general(precond_whole, store_grads, (((1,), (1,)), ((), ())), pre...  7.69 us
  transfers between devices with their start and end apart: 4, of which 4 were waited for; matrix products, arithmetic and copies ran while one was open for 0% of the time, Pallas kernels for 0%

commit v1 on v0

v1 whole, which is shorter than its diff:
```python
import functools
import jax
import jax.numpy as jnp
from jax import lax
from jax.experimental import pallas as pl
from jax.experimental.pallas import tpu as pltpu
from jax.sharding import PartitionSpec as P

F32 = jnp.float32
BF16 = jnp.bfloat16
MESH = pl.DeviceIdType.MESH
CORES = 2
LAGS = (0, 2, 3, 4, 5)
SLOTS = 4


def halves(value):
    high = value.astype(BF16)
    low = (value - high.astype(F32)).astype(BF16)
    return high, low


def dot3(left, right, dims):
    lh, ll = left
    rh, rl = right
    dot = functools.partial(
        lax.dot_general, dimension_numbers=(dims, ((), ())), preferred_element_type=F32
    )
    return dot(lh, rh) + (dot(lh, rl) + dot(ll, rh))


def kernel(
    cfg,
    x_hbm, g_hbm, pin_hbm, pout_hbm, f_hbm, s_hbm, out_ref,
    xin, gin, pin, pout, fbuf, sbuf,
    a_part, a_xrecv, a_xred, a_zrecv, a_full, gt,
    e_all, e_hi, e_lo,
    b_part, b_xrecv, b_xred, b_zrecv, b_full,
    score, srecv,
    in_sem, proj_sem, f_sem, s_sem,
    xs_send, xs_recv, zs_send, zs_recv, zg_send, zg_recv, xg_send, xg_recv,
    ey_send, ey_recv, ec_send, ec_recv, sc_send, sc_recv,
):
    X, Z, T, Y = cfg["X"], cfg["Z"], cfg["T"], cfg["Y"]
    NA, NB, TA, CW, TOK = cfg["NA"], cfg["NB"], cfg["TA"], cfg["CW"], cfg["TOK"]
    S = X * Z
    store, tensor = lax.axis_index("store"), lax.axis_index("tensor")
    mx, mz = lax.rem(store, X), store // X
    my, mc = tensor // CORES, lax.rem(tensor, CORES)
    pj = pin.shape[1]
    pk = pout.shape[1]
    ks = pk // S
    ex_here = xin.shape[0] // TOK
    ex_all = e_all.shape[0]
    ex_chunk = TA // TOK

    def xpeer(d):
        return lax.rem(mx + d, X)

    def zpeer(d):
        return lax.rem(mz + d, Z)

    def to_x(d):
        return {"store": mz * X + xpeer(d), "tensor": tensor}

    def to_z(d):
        return {"store": zpeer(d) * X + mx, "tensor": tensor}

    def to_t(t):
        return {"store": store, "tensor": t}

    def remote(src, dst, send, recv, device):
        return pltpu.make_async_remote_copy(
            src_ref=src, dst_ref=dst, send_sem=send, recv_sem=recv,
            device_id=device, device_id_type=MESH,
        )

    loads = []
    for c in range(NA):
        rows = pl.ds(c * TA, TA)
        loads.append((
            pltpu.make_async_copy(x_hbm.at[rows], xin.at[rows], in_sem.at[c, 0]),
            pltpu.make_async_copy(g_hbm.at[rows], gin.at[rows], in_sem.at[c, 1]),
        ))
    pin_load = pltpu.make_async_copy(pin_hbm, pin, proj_sem.at[0])
    pout_load = pltpu.make_async_copy(pout_hbm, pout, proj_sem.at[1])
    s_load = pltpu.make_async_copy(s_hbm, sbuf, s_sem.at[0])
    pin_load.start()
    pout_load.start()
    for pair in loads:
        pair[0].start()
        pair[1].start()

    def f_load(q):
        slot = q % SLOTS
        return pltpu.make_async_copy(
            f_hbm.at[:, pl.ds(q * CW, CW)], fbuf.at[slot], f_sem.at[slot]
        )

    for q in range(min(SLOTS, NB)):
        f_load(q).start()
    s_load.start()

    barrier = pltpu.get_barrier_semaphore()
    for d in range(1, X):
        pl.semaphore_signal(barrier, inc=1, device_id=to_x(d), device_id_type=MESH)
    for d in range(1, Z):
        pl.semaphore_signal(barrier, inc=1, device_id=to_z(d), device_id_type=MESH)
    for d in range(1, T):
        pl.semaphore_signal(
            barrier, inc=1, device_id=to_t(lax.rem(tensor + d, T)), device_id_type=MESH
        )
    pl.semaphore_wait(barrier, X + Z + T - 3)

    pending = []

    def begin(copy):
        copy.start()
        pending.append(copy)

    def reducer(base, part, xrecv, xred, zrecv, full):
        rows = part.shape[1]
        rx, rz = rows // X, rows // S

        def at_x(p):
            return pl.ds(pl.multiple_of(p * rx, rx), rx)

        def at_z(p):
            return pl.ds(pl.multiple_of(p * rz, rz), rz)

        def at_own(x, z):
            return pl.ds(pl.multiple_of(x * rx + z * rz, rz), rz)

        def x_copy(q, d):
            return remote(part.at[q, at_x(xpeer(d))], xrecv.at[q, d - 1],
                          xs_send.at[base + q, d - 1], xs_recv.at[base + q, d - 1], to_x(d))

        def z_copy(q, d):
            return remote(xred.at[q, at_z(zpeer(d))], zrecv.at[q, d - 1],
                          zs_send.at[base + q, d - 1], zs_recv.at[base + q, d - 1], to_z(d))

        def zg_copy(q, d):
            own = full.at[q, at_own(mx, mz)]
            return remote(own, own, zg_send.at[base + q, d - 1], zg_recv.at[base + q, d - 1], to_z(d))

        def xg_copy(q, d):
            own = full.at[q, at_x(mx)]
            return remote(own, own, xg_send.at[base + q, d - 1], xg_recv.at[base + q, d - 1], to_x(d))

        def send_x(q):
            for d in range(1, X):
                begin(x_copy(q, d))

        def sum_x(q):
            for d in range(1, X):
                x_copy(q, d).wait_recv()
            total = part[q, at_x(mx)]
            for d in range(1, X):
                total += xrecv[q, d - 1]
            xred[q] = total
            for d in range(1, Z):
                begin(z_copy(q, d))

        def sum_z(q):
            for d in range(1, Z):
                z_copy(q, d).wait_recv()
            total = xred[q, at_z(mz)]
            for d in range(1, Z):
                total += zrecv[q, d - 1]
            full[q, at_own(mx, mz)] = total
            for d in range(1, Z):
                begin(zg_copy(q, d))

        def gather_x(q):
            for d in range(1, Z):
                zg_copy(q, d).wait_recv()
            for d in range(1, X):
                begin(xg_copy(q, d))

        def finish(q):
            for d in range(1, X):
                xg_copy(q, d).wait_recv()

        return send_x, sum_x, sum_z, gather_x, finish

    def pipeline(count, stages):
        for tick in range(count + LAGS[-1]):
            for lag, stage in zip(LAGS, stages):
                if 0 <= tick - lag < count:
                    stage(tick - lag)

    send_x, sum_x, sum_z, gather_x, finish = reducer(0, a_part, a_xrecv, a_xred, a_zrecv, a_full)

    def project(c):
        loads[c][0].wait()
        loads[c][1].wait()
        if c == 0:
            pin_load.wait()
            pout_load.wait()
        rows = pl.ds(c * TA, TA)
        a_part[c, :, :pj] = jnp.dot(xin[rows], pin[...], preferred_element_type=F32)
        a_part[c, :, pj:] = jnp.dot(gin[rows], pout[...], preferred_element_type=F32)
        send_x(c)

    def e_rows(t, c):
        return pl.ds(pl.multiple_of(t * ex_here + c * ex_chunk, ex_chunk), ex_chunk)

    def ey_copy(c, d):
        ref = e_all.at[e_rows(tensor, c)]
        other = lax.rem(my + d, Y) * CORES + mc
        return remote(ref, ref, ey_send.at[c, d - 1], ey_recv.at[c, d - 1], to_t(other))

    def ec_copy(c, d):
        source = lax.rem(my + Y - d, Y) * CORES + mc
        ref = e_all.at[e_rows(source, c)]
        return remote(ref, ref, ec_send.at[c, d], ec_recv.at[c, d], to_t(my * CORES + 1 - mc))

    tok_of = lax.broadcasted_iota(jnp.int32, (ex_chunk, TA), 1)
    first = lax.broadcasted_iota(jnp.int32, (ex_chunk, TA), 0) * TOK
    mask = jnp.logical_and(tok_of >= first, tok_of < first + TOK)

    def outer(c):
        finish(c)
        turned = jnp.transpose(a_full[c, :, pj:])
        for block in range(S):
            gt[c, block] = turned[block * ks:(block + 1) * ks]
        mine = gt[c, store]
        wide = jnp.where(mask[None], mine[:, None, :], 0.0).reshape(ks * ex_chunk, TA)
        sums = dot3(halves(wide), halves(a_full[c, :, :pj]), ((1,), (0,)))
        for k in range(ks):
            e_all[e_rows(tensor, c), k * pj:(k + 1) * pj] = sums[k * ex_chunk:(k + 1) * ex_chunk]
        for d in range(1, Y):
            begin(ey_copy(c, d))
        begin(ec_copy(c, 0))

    pipeline(NA, (project, sum_x, sum_z, gather_x, outer))
    for c in range(NA):
        for d in range(1, Y):
            ey_copy(c, d).wait_recv()
            begin(ec_copy(c, d))
    for c in range(NA):
        for d in range(Y):
            ec_copy(c, d).wait_recv()

    depth = e_all.shape[1]
    kt = min(512, depth)

    @pl.loop(0, depth // kt)
    def _(i):
        cols = pl.ds(pl.multiple_of(i * kt, kt), kt)
        high, low = halves(e_all[:, cols])
        e_hi[:, cols] = high
        e_lo[:, cols] = low

    bsend_x, bsum_x, bsum_z, bgather_x, bfinish = reducer(
        NA, b_part, b_xrecv, b_xred, b_zrecv, b_full
    )

    def precondition(q):
        slot = q % SLOTS
        f_load(q).wait()
        b_part[q] = jnp.zeros(b_part.shape[1:], F32)

        @pl.loop(0, depth // kt)
        def _(i):
            cols = pl.ds(pl.multiple_of(i * kt, kt), kt)
            b_part[q] += dot3(
                (e_hi[:, cols], e_lo[:, cols]), halves(fbuf[slot, cols, :]), ((1,), (0,))
            )

        bsend_x(q)
        if q + SLOTS < NB:
            f_load(q + SLOTS).start()

    def add_scores(q):
        bfinish(q)
        if q == 0:
            s_load.wait()
        term = dot3(
            halves(b_full[q]), halves(sbuf[:, pl.ds(q * CW, CW)]), ((1,), (1,))
        )
        if q == 0:
            score[...] = term
        else:
            score[...] += term

    pipeline(NB, (precondition, bsum_x, bsum_z, bgather_x, add_scores))

    def s_rows(t):
        return pl.ds(pl.multiple_of(t * ex_here, ex_here), ex_here)

    def sc_copy(d):
        other = lax.rem(tensor + d, T)
        return remote(score.at[s_rows(other)], srecv.at[d - 1],
                      sc_send.at[d - 1], sc_recv.at[d - 1], to_t(other))

    for d in range(1, T):
        begin(sc_copy(d))
    total = score[s_rows(tensor)]
    for d in range(1, T):
        sc_copy(d).wait_recv()
        total += srecv[d - 1]
    out_ref[...] = total
    for copy in pending:
        copy.wait_send()


def on_device(mesh_shape, inputs, out_grads, proj_in, proj_out, inv_fisher, store_grads):
    T, S = mesh_shape["tensor"], mesh_shape["store"]
    Y = T // CORES
    X = Y if S % Y == 0 else 1
    Z = S // X
    examples, tok, width = inputs.shape
    rows = examples * tok
    flat_inputs = inputs.reshape(rows, width)
    flat_grads = out_grads.reshape(rows, out_grads.shape[2])
    TA = min(rows, max(256, 8 * S))
    NA = rows // TA
    depth, columns = inv_fisher.shape
    CW = min(512, columns)
    NB = columns // CW
    pj, pk = proj_in.shape[1], proj_out.shape[1]
    stored = store_grads.shape[0]
    ex_all = examples * T
    both = pj + pk
    cfg = dict(X=X, Z=Z, T=T, Y=Y, NA=NA, NB=NB, TA=TA, CW=CW, TOK=tok)
    NQ = NA + NB
    dma = pltpu.SemaphoreType.DMA
    vmem = pltpu.VMEM
    scratch = [
        vmem(flat_inputs.shape, BF16), vmem(flat_grads.shape, BF16),
        vmem(proj_in.shape, BF16), vmem(proj_out.shape, BF16),
        vmem((min(SLOTS, NB), depth, CW), F32), vmem(store_grads.shape, F32),
        vmem((NA, TA, both), F32), vmem((NA, X - 1, TA // X, both), F32),
        vmem((NA, TA // X, both), F32), vmem((NA, Z - 1, TA // S, both), F32),
        vmem((NA, TA, both), F32), vmem((NA, S, pk // S, TA), F32),
        vmem((ex_all, depth), F32), vmem((ex_all, depth), BF16), vmem((ex_all, depth), BF16),
        vmem((NB, ex_all, CW), F32), vmem((NB, X - 1, ex_all // X, CW), F32),
        vmem((NB, ex_all // X, CW), F32), vmem((NB, Z - 1, ex_all // S, CW), F32),
        vmem((NB, ex_all, CW), F32),
        vmem((ex_all, stored), F32), vmem((T - 1, examples, stored), F32),
        dma((NA, 2)), dma((2,)), dma((min(SLOTS, NB),)), dma((1,)),
        dma((NQ, X - 1)), dma((NQ, X - 1)), dma((NQ, Z - 1)), dma((NQ, Z - 1)),
        dma((NQ, Z - 1)), dma((NQ, Z - 1)), dma((NQ, X - 1)), dma((NQ, X - 1)),
        dma((NA, max(Y - 1, 1))), dma((NA, max(Y - 1, 1))), dma((NA, Y)), dma((NA, Y)),
        dma((T - 1,)), dma((T - 1,)),
    ]
    hbm = pl.BlockSpec(memory_space=pl.ANY)
    return pl.pallas_call(
        functools.partial(kernel, cfg),
        out_shape=jax.ShapeDtypeStruct((examples, stored), F32),
        in_specs=[hbm] * 6,
        out_specs=pl.BlockSpec(memory_space=pltpu.VMEM),
        scratch_shapes=scratch,
        compiler_params=pltpu.CompilerParams(
            collective_id=0, has_side_effects=True, vmem_limit_bytes=60 * 1024 * 1024
        ),
    )(flat_inputs, flat_grads, proj_in, proj_out, inv_fisher, store_grads)


def solution(mesh):
    placed = (
        P("tensor", None, "store"),
        P("tensor", None, "store"),
        P("store", None),
        P("store", None),
        P("store", "tensor"),
        P("store", "tensor"),
    )
    return jax.shard_map(
        functools.partial(on_device, dict(mesh.shape)), mesh=mesh, in_specs=placed,
        out_specs=P("tensor", "store"), check_vma=False,
    )
```

time: 346 us -> 171 us (0.49)
  waiting for transfers between devices: 279 us -> 0 us
  Pallas kernels: 0 us -> 167 us
  matrix products: 51.6 us -> 0 us
  between operations: 13.1 us -> 0.01 us
    psum x2 -> x0, waiting for transfers between devices: 237 us -> none  [the longest x1 156 us: on_device(): precond_whole = lax.psum(precond_part, 'store')]
    pallas_call x0 -> x1, Pallas kernels: none -> 167 us  [on_device(): pl.pallas_call(functools.partial(kernel, cfg), out_shape=jax.ShapeDtypeSt...]
    dot_general x5 -> x0, matrix products: 51.6 us -> none  [the longest x1 34 us: on_device(): jnp.dot(lax.all_gather(local_grads, 'tensor', axis=0, tiled=True), inv_fi...]
    all_gather x1 -> x0, waiting for transfers between devices: 22.1 us -> none  [on_device(): lax.all_gather(local_grads, 'tensor', axis=0, tiled=True)]
    reduce_scatter x1 -> x0, waiting for transfers between devices: 19.2 us -> none  [on_device(): lax.psum_scatter(partial_scores, 'tensor', scatter_dimension=0, tiled=True)]
  transfers between devices with their start and end apart: 4 -> 0, of which waited for: 4 -> 0; matrix products, arithmetic and copies ran while one was open for 0% -> 0% of each run, Pallas kernels for 0% -> 0%
where the time goes in v1:
time: 171 us; the launch traced here: 168 us
  Pallas kernels  167 us (98%)
    pallas_call x1, Pallas kernels, on_device(): pl.pallas_call(functools.partial(kernel, cfg), out_shape=jax.ShapeDtypeSt...  167 us

profile of v1, /device:TPU:0, one launch (start us, length us, event | category | flops | bytes accessed | tf_op | source)
XLA Modules:
  0.0 168.3 jit_solution(7917557895874880670)
XLA Ops:
  0.0 166.8 %shard_map.64 = f32[64,256]{1,0:T(8,128)} custom-call(bf16[1024,3584]{1,0:T(8,128)(2,1)} %bitcast.2, bf16[1024,1024]{1,0:T(8,128)(2,1)} %bitcast.3, bf16[3584,128]{1,0:T(8,128)(2,1)} %pin_hbm.1, bf16[1024,128]{1,0:T(8,128)(2,1)} %pout_hbm.1, f32[2048,4096]{1,0:T(8,128)} %f_hbm.1, f32[256,4096]{1,0:T(8,128)} %s_hbm.1), custom_call_target="tpu_custom_call" | custom-call | tf_op jit(solution)/shard_map/pallas_call | solution.py:349
  166.8 1.5 copy.8

commit v2 on v1

v2 whole, which is shorter than its diff:
```python
import functools
import jax
import jax.numpy as jnp
from jax import lax
from jax.experimental import pallas as pl
from jax.experimental.pallas import tpu as pltpu
from jax.sharding import PartitionSpec as P

F32 = jnp.float32
BF16 = jnp.bfloat16
MESH = pl.DeviceIdType.MESH
CORES = 2
A_LAGS = (0, 1, 2, 3, 4, 5)
B_LAGS = (0, 2, 3, 4, 5)
SLOTS = 4


def halves(value):
    high = value.astype(BF16)
    low = (value - high.astype(F32)).astype(BF16)
    return high, low


def dot3(left, right, dims):
    lh, ll = left
    rh, rl = right
    dot = functools.partial(
        lax.dot_general, dimension_numbers=(dims, ((), ())), preferred_element_type=F32
    )
    return dot(lh, rh) + (dot(lh, rl) + dot(ll, rh))


def kernel(
    cfg,
    x_hbm, g_hbm, pin_hbm, pout_hbm, f_hbm, s_hbm, out_ref,
    xin, gin, pin, pout, fbuf, sbuf,
    a_part, a_xrecv, a_red, a_zrecv, a_full, gt,
    e_all, e_hi, e_lo,
    b_part, b_xrecv, b_red, b_zrecv, b_full,
    score, trecv, xpart, xrecv,
    in_sem, proj_sem, f_sem, s_sem,
    xs_send, xs_recv, zs_send, zs_recv, zg_send, zg_recv, xg_send, xg_recv,
    ey_send, ey_recv, ec_send, ec_recv, st_send, st_recv, sc_send, sc_recv, sx_send, sx_recv,
):
    X, Z, T, Y = cfg["X"], cfg["Z"], cfg["T"], cfg["Y"]
    NA, NB, TA, CW, TOK = cfg["NA"], cfg["NB"], cfg["TA"], cfg["CW"], cfg["TOK"]
    S = X * Z
    store, tensor = lax.axis_index("store"), lax.axis_index("tensor")
    mx, mz = lax.rem(store, X), store // X
    my, mc = tensor // CORES, lax.rem(tensor, CORES)
    pj = pin.shape[1]
    pk = pout.shape[1]
    ks = pk // S
    ex_here = xin.shape[0] // TOK
    ex_all = e_all.shape[0]
    ex_chunk = TA // TOK

    def xpeer(d):
        return lax.rem(mx + d, X)

    def zpeer(d):
        return lax.rem(mz + d, Z)

    def to_x(d):
        return {"store": mz * X + xpeer(d), "tensor": tensor}

    def to_z(d):
        return {"store": zpeer(d) * X + mx, "tensor": tensor}

    def to_t(t):
        return {"store": store, "tensor": t}

    def remote(src, dst, send, recv, device):
        return pltpu.make_async_remote_copy(
            src_ref=src, dst_ref=dst, send_sem=send, recv_sem=recv,
            device_id=device, device_id_type=MESH,
        )

    loads = []
    for c in range(NA):
        rows = pl.ds(c * TA, TA)
        loads.append((
            pltpu.make_async_copy(x_hbm.at[rows], xin.at[rows], in_sem.at[c, 0]),
            pltpu.make_async_copy(g_hbm.at[rows], gin.at[rows], in_sem.at[c, 1]),
        ))
    pin_load = pltpu.make_async_copy(pin_hbm, pin, proj_sem.at[0])
    pout_load = pltpu.make_async_copy(pout_hbm, pout, proj_sem.at[1])
    CX = s_hbm.shape[1] // X
    WX = CW // X

    def s_columns(x, q):
        return pl.ds(pl.multiple_of(x * CX + q * WX, WX), WX)

    def s_load(q):
        return pltpu.make_async_copy(
            s_hbm.at[:, s_columns(mx, q)], sbuf.at[q, mx], s_sem.at[q]
        )

    def s_copy(q, d):
        return remote(s_hbm.at[:, s_columns(xpeer(d), q)], sbuf.at[q, mx],
                      st_send.at[q, d - 1], st_recv.at[q, d - 1], to_x(d))

    def s_arrival(q, d):
        source = lax.rem(mx + X - d, X)
        return remote(sbuf.at[q, source], sbuf.at[q, source],
                      st_send.at[q, d - 1], st_recv.at[q, d - 1], to_x(d))

    pin_load.start()
    pout_load.start()
    for pair in loads:
        pair[0].start()
        pair[1].start()

    def f_load(q, x):
        slot = q % SLOTS
        return pltpu.make_async_copy(
            f_hbm.at[:, pl.ds(x * CX + q * WX, WX)], fbuf.at[slot, x], f_sem.at[slot, x]
        )

    for q in range(min(SLOTS, NB)):
        for x in range(X):
            f_load(q, x).start()
    for q in range(NB):
        s_load(q).start()

    barrier = pltpu.get_barrier_semaphore()
    for d in range(1, X):
        pl.semaphore_signal(barrier, inc=1, device_id=to_x(d), device_id_type=MESH)
    for d in range(1, Z):
        pl.semaphore_signal(barrier, inc=1, device_id=to_z(d), device_id_type=MESH)
    for d in range(1, T):
        pl.semaphore_signal(
            barrier, inc=1, device_id=to_t(lax.rem(tensor + d, T)), device_id_type=MESH
        )
    pl.semaphore_wait(barrier, X + Z + T - 3)

    pending = []

    def begin(copy):
        copy.start()
        pending.append(copy)

    half = Z // 2
    lower = mz < half
    inward = jnp.where(lower, mz + 1, mz - 1)
    outward = jnp.where(lower, mz - 1, mz + 1)
    from_middle = jnp.where(lower, half - 1 - mz, mz - half)
    is_middle = from_middle == 0
    is_end = from_middle == half - 1
    slot_there = jnp.where(is_middle, 1, 0)
    to_in = {"store": inward * X + mx, "tensor": tensor}
    to_out = {"store": outward * X + mx, "tensor": tensor}
    finals = []

    def tree(base, red, zrecv, result):
        def inward_copy(q):
            return remote(red.at[q], zrecv.at[q, slot_there],
                          zs_send.at[base + q], zs_recv.at[base + q, slot_there], to_in)

        def arrival(q, slot):
            return remote(red.at[q], zrecv.at[q, slot],
                          zs_send.at[base + q], zs_recv.at[base + q, slot], to_in)

        def outward_copy(q):
            return remote(result(q), result(q), zg_send.at[base + q], zg_recv.at[base + q], to_out)

        def enter(q):
            @pl.when(is_end)
            def _():
                inward_copy(q).start()

        def up(q):
            @pl.when(jnp.logical_not(is_end))
            def _():
                arrival(q, 0).wait_recv()
                red[q] += zrecv[q, 0]
                inward_copy(q).start()

        def middle(q):
            @pl.when(is_middle)
            def _():
                arrival(q, 1).wait_recv()
                result(q)[...] = red[q] + zrecv[q, 1]
                if half > 1:
                    outward_copy(q).start()

        def down(q):
            @pl.when(jnp.logical_not(is_middle))
            def _():
                outward_copy(q).wait_recv()

                @pl.when(jnp.logical_not(is_end))
                def _():
                    outward_copy(q).start()

        def drain(count):
            for q in range(count):
                inward_copy(q).wait_send()

            @pl.when(jnp.logical_not(is_end))
            def _():
                for q in range(count):
                    outward_copy(q).wait_send()

        finals.append(drain)
        return enter, up, middle, down

    def pipeline(count, lags, stages, beside=None):
        for tick in range(count + lags[-1]):
            for lag, stage in zip(lags, stages):
                if 0 <= tick - lag < count:
                    stage(tick - lag)
            if beside is not None:
                beside(tick)

    rx = TA // X

    def at_x(p):
        return pl.ds(pl.multiple_of(p * rx, rx), rx)

    def a_total(c):
        return a_full.at[c, at_x(mx)]

    a_enter, a_up, a_middle, a_down = tree(0, a_red, a_zrecv, a_total)

    def ax_copy(c, d):
        return remote(a_part.at[c, at_x(xpeer(d))], a_xrecv.at[c, d - 1],
                      xs_send.at[c, d - 1], xs_recv.at[c, d - 1], to_x(d))

    def xg_copy(c, d):
        return remote(a_total(c), a_total(c),
                      xg_send.at[c, d - 1], xg_recv.at[c, d - 1], to_x(d))

    def a_sum_x(c):
        for d in range(1, X):
            ax_copy(c, d).wait_recv()
        total = a_part[c, at_x(mx)]
        for d in range(1, X):
            total += a_xrecv[c, d - 1]
        a_red[c] = total
        a_enter(c)

    def a_gather_x(c):
        a_down(c)
        for d in range(1, X):
            begin(xg_copy(c, d))

    def project(c):
        loads[c][0].wait()
        loads[c][1].wait()
        if c == 0:
            pin_load.wait()
            pout_load.wait()
        rows = pl.ds(c * TA, TA)
        a_part[c, :, :pj] = jnp.dot(xin[rows], pin[...], preferred_element_type=F32)
        a_part[c, :, pj:] = jnp.dot(gin[rows], pout[...], preferred_element_type=F32)
        for d in range(1, X):
            begin(ax_copy(c, d))

    def e_rows(t, c):
        return pl.ds(pl.multiple_of(t * ex_here + c * ex_chunk, ex_chunk), ex_chunk)

    def ey_copy(c, d):
        ref = e_all.at[e_rows(tensor, c)]
        other = lax.rem(my + d, Y) * CORES + mc
        return remote(ref, ref, ey_send.at[c, d - 1], ey_recv.at[c, d - 1], to_t(other))

    def ec_copy(c, d):
        source = lax.rem(my + Y - d, Y) * CORES + mc
        ref = e_all.at[e_rows(source, c)]
        return remote(ref, ref, ec_send.at[c, d], ec_recv.at[c, d], to_t(my * CORES + 1 - mc))

    tok_of = lax.broadcasted_iota(jnp.int32, (ex_chunk, TA), 1)
    first = lax.broadcasted_iota(jnp.int32, (ex_chunk, TA), 0) * TOK
    mask = jnp.logical_and(tok_of >= first, tok_of < first + TOK)

    def outer(c):
        for d in range(1, X):
            xg_copy(c, d).wait_recv()
        turned = jnp.transpose(a_full[c, :, pj:])
        for block in range(S):
            gt[c, block] = turned[block * ks:(block + 1) * ks]
        mine = gt[c, store]
        wide = jnp.where(mask[None], mine[:, None, :], 0.0).reshape(ks * ex_chunk, TA)
        sums = dot3(halves(wide), halves(a_full[c, :, :pj]), ((1,), (0,)))
        for k in range(ks):
            e_all[e_rows(tensor, c), k * pj:(k + 1) * pj] = sums[k * ex_chunk:(k + 1) * ex_chunk]
        for d in range(1, Y):
            begin(ey_copy(c, d))
        begin(ec_copy(c, 0))

    def store_columns(tick):
        if tick >= A_LAGS[1] and tick - A_LAGS[1] < NB:
            for d in range(1, X):
                begin(s_copy(tick - A_LAGS[1], d))

    pipeline(NA, A_LAGS, (project, a_sum_x, a_up, a_middle, a_gather_x, outer), store_columns)
    for q in range(NA + A_LAGS[-1] - A_LAGS[1], NB):
        for d in range(1, X):
            begin(s_copy(q, d))
    for c in range(NA):
        for d in range(1, Y):
            ey_copy(c, d).wait_recv()
            begin(ec_copy(c, d))
    for c in range(NA):
        for d in range(Y):
            ec_copy(c, d).wait_recv()

    depth = e_all.shape[1]
    kt = min(512, depth)

    @pl.loop(0, depth // kt)
    def _(i):
        cols = pl.ds(pl.multiple_of(i * kt, kt), kt)
        high, low = halves(e_all[:, cols])
        e_hi[:, cols] = high
        e_lo[:, cols] = low

    b_enter, b_up, b_middle, b_down = tree(NA, b_red, b_zrecv, lambda q: b_full.at[q])

    def bx_copy(q, d):
        return remote(b_part.at[q, xpeer(d)], b_xrecv.at[q, d - 1],
                      xs_send.at[NA + q, d - 1], xs_recv.at[NA + q, d - 1], to_x(d))

    def precondition(q):
        slot = q % SLOTS
        for x in range(X):
            f_load(q, x).wait()
        for x in range(X):
            b_part[q, x] = jnp.zeros(b_part.shape[2:], F32)

            @pl.loop(0, depth // kt)
            def _(i):
                cols = pl.ds(pl.multiple_of(i * kt, kt), kt)
                b_part[q, x] += dot3(
                    (e_hi[:, cols], e_lo[:, cols]), halves(fbuf[slot, x, cols, :]), ((1,), (0,))
                )

        for d in range(1, X):
            begin(bx_copy(q, d))
        if q + SLOTS < NB:
            for x in range(X):
                f_load(q + SLOTS, x).start()

    def b_sum_x(q):
        for d in range(1, X):
            bx_copy(q, d).wait_recv()
        total = b_part[q, mx]
        for d in range(1, X):
            total += b_xrecv[q, d - 1]
        b_red[q] = total
        b_enter(q)

    def add_scores(q):
        b_down(q)
        s_load(q).wait()
        for d in range(1, X):
            s_arrival(q, d).wait_recv()
        left = halves(b_full[q])
        for x in range(X):
            term = dot3(left, halves(sbuf[q, x]), ((1,), (1,)))
            if q == 0:
                score[x] = term
            else:
                score[x] += term

    pipeline(NB, B_LAGS, (precondition, b_sum_x, b_up, b_middle, add_scores))

    def s_rows(t):
        return pl.ds(pl.multiple_of(t * ex_here, ex_here), ex_here)

    def sc_copy(d):
        other = lax.rem(tensor + d, T)
        return remote(score.at[:, s_rows(other)], trecv.at[d - 1],
                      sc_send.at[d - 1], sc_recv.at[d - 1], to_t(other))

    def sx_copy(d):
        return remote(xpart.at[xpeer(d)], xrecv.at[d - 1],
                      sx_send.at[d - 1], sx_recv.at[d - 1], to_x(d))

    for d in range(1, T):
        begin(sc_copy(d))
    total = score[:, s_rows(tensor)]
    for d in range(1, T):
        sc_copy(d).wait_recv()
        total += trecv[d - 1]
    xpart[...] = total
    for d in range(1, X):
        begin(sx_copy(d))
    total = xpart[mx]
    for d in range(1, X):
        sx_copy(d).wait_recv()
        total += xrecv[d - 1]
    out_ref[...] = total
    finals[0](NA)
    finals[1](NB)
    for copy in pending:
        copy.wait_send()


def on_device(mesh_shape, inputs, out_grads, proj_in, proj_out, inv_fisher, store_grads):
    T, S = mesh_shape["tensor"], mesh_shape["store"]
    Y = T // CORES
    X = Y if S % Y == 0 else 1
    Z = S // X
    examples, tok, width = inputs.shape
    rows = examples * tok
    flat_inputs = inputs.reshape(rows, width)
    flat_grads = out_grads.reshape(rows, out_grads.shape[2])
    TA = min(rows, max(256, 8 * S))
    NA = rows // TA
    depth, columns = inv_fisher.shape
    CW = min(512, columns)
    NB = columns // CW
    pj, pk = proj_in.shape[1], proj_out.shape[1]
    stored = store_grads.shape[0]
    ex_all = examples * T
    both = pj + pk
    cfg = dict(X=X, Z=Z, T=T, Y=Y, NA=NA, NB=NB, TA=TA, CW=CW, TOK=tok)
    NQ = NA + NB
    dma = pltpu.SemaphoreType.DMA
    vmem = pltpu.VMEM
    scratch = [
        vmem(flat_inputs.shape, BF16), vmem(flat_grads.shape, BF16),
        vmem(proj_in.shape, BF16), vmem(proj_out.shape, BF16),
        vmem((min(SLOTS, NB), X, depth, CW // X), F32),
        vmem((NB, X, stored, CW // X), F32),
        vmem((NA, TA, both), F32), vmem((NA, X - 1, TA // X, both), F32),
        vmem((NA, TA // X, both), F32), vmem((NA, 2, TA // X, both), F32),
        vmem((NA, TA, both), F32), vmem((NA, S, pk // S, TA), F32),
        vmem((ex_all, depth), F32), vmem((ex_all, depth), BF16), vmem((ex_all, depth), BF16),
        vmem((NB, X, ex_all, CW // X), F32), vmem((NB, X - 1, ex_all, CW // X), F32),
        vmem((NB, ex_all, CW // X), F32), vmem((NB, 2, ex_all, CW // X), F32),
        vmem((NB, ex_all, CW // X), F32),
        vmem((X, ex_all, stored), F32), vmem((T - 1, X, examples, stored), F32),
        vmem((X, examples, stored), F32), vmem((X - 1, examples, stored), F32),
        dma((NA, 2)), dma((2,)), dma((min(SLOTS, NB), X)), dma((NB,)),
        dma((NQ, X - 1)), dma((NQ, X - 1)), dma((NQ,)), dma((NQ, 2)),
        dma((NQ,)), dma((NQ,)), dma((NA, X - 1)), dma((NA, X - 1)),
        dma((NA, max(Y - 1, 1))), dma((NA, max(Y - 1, 1))), dma((NA, Y)), dma((NA, Y)),
        dma((NB, X - 1)), dma((NB, X - 1)), dma((T - 1,)), dma((T - 1,)),
        dma((X - 1,)), dma((X - 1,)),
    ]
    hbm = pl.BlockSpec(memory_space=pl.ANY)
    return pl.pallas_call(
        functools.partial(kernel, cfg),
        out_shape=jax.ShapeDtypeStruct((examples, stored), F32),
        in_specs=[hbm] * 6,
        out_specs=pl.BlockSpec(memory_space=pltpu.VMEM),
        scratch_shapes=scratch,
        compiler_params=pltpu.CompilerParams(
            collective_id=0, has_side_effects=True, vmem_limit_bytes=60 * 1024 * 1024
        ),
    )(flat_inputs, flat_grads, proj_in, proj_out, inv_fisher, store_grads)


def solution(mesh):
    placed = (
        P("tensor", None, "store"),
        P("tensor", None, "store"),
        P("store", None),
        P("store", None),
        P("store", "tensor"),
        P("store", "tensor"),
    )
    return jax.shard_map(
        functools.partial(on_device, dict(mesh.shape)), mesh=mesh, in_specs=placed,
        out_specs=P("tensor", "store"), check_vma=False,
    )
```

time: 171 us -> 163 us (0.953); the launches traced: 168 us -> 163 us
  Pallas kernels: 167 us -> 161 us
    pallas_call x1, Pallas kernels: 167 us -> 161 us  [on_device(): pl.pallas_call(functools.partial(kernel, cfg), out_shape=jax.ShapeDtypeSt...]
where the time goes in v2:
time: 163 us
  Pallas kernels  161 us (99%)
    pallas_call x1, Pallas kernels, on_device(): pl.pallas_call(functools.partial(kernel, cfg), out_shape=jax.ShapeDtypeSt...  161 us

profile of v2, /device:TPU:0, one launch (start us, length us, event | category | flops | bytes accessed | tf_op | source)
XLA Modules:
  0.0 162.9 jit_solution(15699517471558202213)
XLA Ops:
  0.0 161.5 %shard_map.64 = f32[64,256]{1,0:T(8,128)} custom-call(bf16[1024,3584]{1,0:T(8,128)(2,1)} %bitcast.2, bf16[1024,1024]{1,0:T(8,128)(2,1)} %bitcast.3, bf16[3584,128]{1,0:T(8,128)(2,1)} %pin_hbm.1, bf16[1024,128]{1,0:T(8,128)(2,1)} %pout_hbm.1, f32[2048,4096]{1,0:T(8,128)} %f_hbm.1, f32[256,4096]{1,0:T(8,128)} %s_hbm.1), custom_call_target="tpu_custom_call" | custom-call | tf_op jit(solution)/shard_map/pallas_call | solution.py:445
  161.5 1.5 copy.8

commit v3 on v2

--- a/solution.py
+++ b/solution.py
@@ -13,6 +13,7 @@
 A_LAGS = (0, 1, 2, 3, 4, 5)
 B_LAGS = (0, 2, 3, 4, 5)
 SLOTS = 4
+EARLY = 2
 
 
 def halves(value):
@@ -290,12 +291,16 @@
         begin(ec_copy(c, 0))
 
     def store_columns(tick):
-        if tick >= A_LAGS[1] and tick - A_LAGS[1] < NB:
+        if EARLY <= tick + EARLY < NB:
             for d in range(1, X):
-                begin(s_copy(tick - A_LAGS[1], d))
+                begin(s_copy(tick + EARLY, d))
+
+    for q in range(min(EARLY, NB)):
+        for d in range(1, X):
+            begin(s_copy(q, d))
 
     pipeline(NA, A_LAGS, (project, a_sum_x, a_up, a_middle, a_gather_x, outer), store_columns)
-    for q in range(NA + A_LAGS[-1] - A_LAGS[1], NB):
+    for q in range(NA + A_LAGS[-1] + EARLY, NB):
         for d in range(1, X):
             begin(s_copy(q, d))
     for c in range(NA):

time: 163 us -> 166 us (1.018)
  Pallas kernels: 161 us -> 164 us
    pallas_call x1, Pallas kernels: 161 us -> 164 us  [on_device(): pl.pallas_call(functools.partial(kernel, cfg), out_shape=jax.ShapeDtypeSt...]
where the time goes in v3:
time: 166 us
  Pallas kernels  164 us (99%)
    pallas_call x1, Pallas kernels, on_device(): pl.pallas_call(functools.partial(kernel, cfg), out_shape=jax.ShapeDtypeSt...  164 us

profile of v3, /device:TPU:0, one launch (start us, length us, event | category | flops | bytes accessed | tf_op | source)
XLA Modules:
  0.0 165.9 jit_solution(4478210362132857307)
XLA Ops:
  0.0 164.4 %shard_map.64 = f32[64,256]{1,0:T(8,128)} custom-call(bf16[1024,3584]{1,0:T(8,128)(2,1)} %bitcast.2, bf16[1024,1024]{1,0:T(8,128)(2,1)} %bitcast.3, bf16[3584,128]{1,0:T(8,128)(2,1)} %pin_hbm.1, bf16[1024,128]{1,0:T(8,128)(2,1)} %pout_hbm.1, f32[2048,4096]{1,0:T(8,128)} %f_hbm.1, f32[256,4096]{1,0:T(8,128)} %s_hbm.1), custom_call_target="tpu_custom_call" | custom-call | tf_op jit(solution)/shard_map/pallas_call | solution.py:450
  164.4 1.5 copy.8
